TPU v7x, 256 devices: a whole 4x4x8 slice. The times are simulated.
256 devices in a mesh: dp: 8 (over z), ctx: 32 (over y, x, core).
Axes of the slice: x: 4, y: 4, z: 8, core: 2. Of those that a mesh axis runs over, the one named last changes fastest.
Arguments:
- output_gate_input: bfloat16 [8, 4096, 4096], P('dp', 'ctx'), may hold values from -6 to 6
- key_input: bfloat16 [8, 4096, 4096], P('dp', 'ctx'), may hold values from -6 to 6
- value_input: bfloat16 [8, 4096, 4096], P('dp', 'ctx'), may hold values from -6 to 6
- upstream: bfloat16 [8, 4096, 4096], P('dp', 'ctx'), may hold values from -6 to 6
- filter_taps: float32 [256, 4096], P('ctx'), may hold values from -6 to 6
- block_of_shard: int32 [32], replicated, may hold values from 0 to 31, each once
Outputs:
- mixed_out: bfloat16 [8, 4096, 4096], P('dp', 'ctx')
- gate_grad: bfloat16 [8, 4096, 4096], P('dp', 'ctx')
- key_grad: bfloat16 [8, 4096, 4096], P('dp', 'ctx')
- value_grad: bfloat16 [8, 4096, 4096], P('dp', 'ctx')
- taps_grad: float32 [256, 4096], P('ctx')
Inputs may be any that keep to these rules, and one draw needn't show every extreme that they name: block_of_shard names every block of positions exactly once.
All inputs are finite; a program needn't handle non-finite values.
Results may differ from a plain program's by a relative error of at most 0.012.
Values may be sent and summed in bfloat16 or wider, within the bound.
No kernel may reach another device: no remote copies, remote signals or barrier semaphores. Data moves between devices by JAX's collectives and lax.ppermute only.
A program may use at most 192 MiB of HBM per device.

v0:
```python
import math
import jax
import jax.numpy as jnp
from jax import lax
from jax.sharding import PartitionSpec as P

epsilon = 1e-06


def inverse_order(block_of_shard):
    pieces = block_of_shard.shape[0]
    labels = jnp.arange(pieces, dtype=jnp.int32)
    matches = (block_of_shard[:, None] == labels[None, :]).astype(jnp.int32)
    return jnp.sum(labels[:, None] * matches, axis=0)


def reorder_blocks(row_data, placing):
    pieces = placing.shape[0]
    shaped = row_data.reshape((pieces, row_data.shape[0] // pieces) + row_data.shape[1:])
    return jnp.take(shaped, placing, axis=0).reshape(row_data.shape)


def toeplitz_tables(kernel, block_rows):
    groups, length = kernel.shape
    pieces = length // block_rows
    padded = jnp.concatenate([jnp.zeros((groups, block_rows), kernel.dtype), kernel], axis=1)
    padded = padded.reshape(groups, pieces + 1, block_rows)
    tables = []
    for lag_block in range(pieces):
        segment = jnp.concatenate([padded[:, lag_block], padded[:, lag_block + 1]], axis=1)
        turned = jnp.roll(segment[:, ::-1], -(block_rows - 1), axis=1)
        flat = jnp.tile(turned, (1, block_rows))[:, : block_rows * (2 * block_rows - 1)]
        tables.append(flat.reshape(groups, block_rows, 2 * block_rows - 1)[:, :, :block_rows])
    return tables


def diagonal_sums(square):
    groups, block_rows, _ = square.shape
    flipped = square[:, :, ::-1]
    padded = jnp.pad(flipped, ((0, 0), (0, 0), (0, block_rows + 1)))
    flat = padded.reshape(groups, block_rows * (2 * block_rows + 1))[
        :, : 2 * block_rows * block_rows
    ]
    return jnp.sum(flat.reshape(groups, block_rows, 2 * block_rows), axis=1)


def forward_part(tables, signal, groups, block_rows):
    length, channels = signal.shape
    pieces = length // block_rows
    blocks = signal.reshape(pieces, block_rows, groups, channels // groups)
    total = jnp.zeros(blocks.shape, jnp.float32)
    for lag_block in range(pieces):
        contrib = jnp.einsum(
            "grs,jsgc->jrgc",
            tables[lag_block],
            blocks[: pieces - lag_block],
            preferred_element_type=jnp.float32,
        )
        total = total + jnp.pad(contrib, ((lag_block, 0), (0, 0), (0, 0), (0, 0)))
    return total.reshape(length, channels).astype(jnp.bfloat16)


def backward_part(tables, signal, weighted_seq, groups, block_rows):
    length, channels = signal.shape
    pieces = length // block_rows
    blocks = signal.reshape(pieces, block_rows, groups, channels // groups)
    wblocks = weighted_seq.reshape(pieces, block_rows, groups, channels // groups)
    total = jnp.zeros(blocks.shape, jnp.float32)
    lag_buffer = jnp.zeros((groups, (pieces + 1) * block_rows), jnp.float32)
    for lag_block in range(pieces):
        later = wblocks[lag_block:]
        contrib = jnp.einsum(
            "grs,jrgc->jsgc", tables[lag_block], later, preferred_element_type=jnp.float32
        )
        total = total + jnp.pad(contrib, ((0, lag_block), (0, 0), (0, 0), (0, 0)))
        square = jnp.einsum(
            "jrgc,jsgc->grs",
            later,
            blocks[: pieces - lag_block],
            preferred_element_type=jnp.float32,
        )
        folded = diagonal_sums(square)[:, : 2 * block_rows - 1]
        start = lag_block * block_rows + 1
        lag_buffer = lag_buffer + jnp.pad(
            folded, ((0, 0), (start, (pieces + 1) * block_rows - start - 2 * block_rows + 1))
        )
    returned = total.reshape(length, channels).astype(jnp.bfloat16)
    return (returned, lag_buffer[:, block_rows : block_rows + length])


def gate_product(first, second):
    return (first.astype(jnp.float32) * second.astype(jnp.float32)).astype(jnp.bfloat16)


def shards(output_gate_input, key_input, value_input, upstream, filter_taps, block_of_shard):
    inverse = inverse_order(block_of_shard)
    groups, length = filter_taps.shape
    block_rows = min(length, max(256, length // 16))
    root_mean = jnp.sqrt(jnp.mean(filter_taps * filter_taps, axis=1, keepdims=True) + epsilon)
    norm_scale = 1.0 / (math.sqrt(length) * root_mean)
    kernel = (filter_taps * norm_scale).astype(jnp.bfloat16)
    tables = toeplitz_tables(kernel, block_rows)
    gates_here = output_gate_input[0]
    keys_here = key_input[0]
    values_here = value_input[0]
    upstream_here = upstream[0]
    product = gate_product(keys_here, values_here)
    arrived = (
        lax.all_to_all(product, "ctx", split_axis=1, concat_axis=0, tiled=True),
        lax.all_to_all(gates_here, "ctx", split_axis=1, concat_axis=0, tiled=True),
        lax.all_to_all(upstream_here, "ctx", split_axis=1, concat_axis=0, tiled=True),
    )
    signal = reorder_blocks(arrived[0], inverse)
    gates_seq = reorder_blocks(arrived[1], inverse)
    upstream_seq = reorder_blocks(arrived[2], inverse)
    mixing = forward_part(tables, signal, groups, block_rows)
    weighted_seq = gate_product(upstream_seq, gates_seq)
    returned, lag_sums = backward_part(tables, signal, weighted_seq, groups, block_rows)
    mixed_seq = reorder_blocks(gate_product(gates_seq, mixing), block_of_shard)
    gate_seq = reorder_blocks(gate_product(upstream_seq, mixing), block_of_shard)
    returned = reorder_blocks(returned, block_of_shard)
    mixed_out, gate_grad, returned_here = (
        lax.all_to_all(mixed_seq, "ctx", split_axis=0, concat_axis=1, tiled=True),
        lax.all_to_all(gate_seq, "ctx", split_axis=0, concat_axis=1, tiled=True),
        lax.all_to_all(returned, "ctx", split_axis=0, concat_axis=1, tiled=True),
    )
    key_grad = gate_product(returned_here, values_here)
    value_grad = gate_product(returned_here, keys_here)
    lag_total = lax.psum(lag_sums, "dp")
    lag_mean = lag_total / lax.axis_size("dp")
    projection = jnp.sum(lag_mean * filter_taps, axis=1, keepdims=True)
    taps_grad = (
        norm_scale * lag_mean - filter_taps * (norm_scale * norm_scale * norm_scale) * projection
    )
    return (mixed_out[None], gate_grad[None], key_grad[None], value_grad[None], taps_grad)


def solution(mesh):
    return jax.shard_map(
        shards,
        mesh=mesh,
        in_specs=(
            P("dp", "ctx", None),
            P("dp", "ctx", None),
            P("dp", "ctx", None),
            P("dp", "ctx", None),
            P("ctx", None),
            P(),
        ),
        out_specs=(
            P("dp", "ctx", None),
            P("dp", "ctx", None),
            P("dp", "ctx", None),
            P("dp", "ctx", None),
            P("ctx", None),
        ),
        check_vma=False,
    )
```

profile of v0, /device:TPU:1, one launch (start us, length us, event | category | flops | bytes accessed | tf_op | source)
XLA Modules:
  0.0 1130.7 jit_solution(15635006254996681494)
XLA Ops:
  11.2 8.7 all-to-all-start.1
  21.9 15.2 %all-to-all-done.1 = bf16[128,32,128]{2,0,1:T(8,128)(2,1)S(1)} async-done(((bf16[128,32,128]{2,0,1:T(8,128)(2,1)}), bf16[128,32,128]{2,0,1:T(8,128)(2,1)S(1)}, u32[]{:S(2)}, u32[]{:S(2)}) %all-to-all-start.1) | async-done | bytes 1048608 | tf_op jit(solution)/shard_map/all_to_all | solution.py:109
  44.1 14.2 %all-to-all-done = bf16[128,32,128]{2,0,1:T(8,128)(2,1)S(1)} async-done(((bf16[128,32,128]{2,0,1:T(8,128)(2,1)}), bf16[128,32,128]{2,0,1:T(8,128)(2,1)S(1)}, u32[]{:S(2)}, u32[]{:S(2)}) %all-to-all-start) | async-done | bytes 1048608 | tf_op jit(solution)/shard_map/all_to_all | solution.py:110
  68.2 12.2 %all-to-all-done.3 = bf16[128,32,128]{2,0,1:T(8,128)(2,1)} async-done(((bf16[128,32,128]{2,0,1:T(8,128)(2,1)}), bf16[128,32,128]{2,0,1:T(8,128)(2,1)}, u32[]{:S(2)}, u32[]{:S(2)}) %all-to-all-start.3) | async-done | bytes 1048608 | tf_op jit(solution)/shard_map/all_to_all | solution.py:111
  151.3 17.5 %rev.65 = f32[8,256,256]{2,1,0:T(8,128)} reverse(f32[8,256,256]{2,1,0:T(8,128)} %convolution_bitcast_fusion.10), dimensions={2} | reverse | bytes 4194304 | tf_op jit(solution)/shard_map/rev | solution.py:39
  170.7 17.7 %rev.64 = f32[8,256,256]{2,1,0:T(8,128)} reverse(f32[8,256,256]{2,1,0:T(8,128)} %convolution_bitcast_fusion.11), dimensions={2} | reverse | bytes 4194304 | tf_op jit(solution)/shard_map/rev | solution.py:39
  190.2 17.7 %rev.66 = f32[8,256,256]{2,1,0:T(8,128)} reverse(f32[8,256,256]{2,1,0:T(8,128)} %convolution_bitcast_fusion.9), dimensions={2} | reverse | bytes 4194304 | tf_op jit(solution)/shard_map/rev | solution.py:39
  209.7 17.7 %rev.67 = f32[8,256,256]{2,1,0:T(8,128)} reverse(f32[8,256,256]{2,1,0:T(8,128)} %convolution_bitcast_fusion.8), dimensions={2} | reverse | bytes 4194304 | tf_op jit(solution)/shard_map/rev | solution.py:39
  229.2 17.7 %rev.68 = f32[8,256,256]{2,1,0:T(8,128)} reverse(f32[8,256,256]{2,1,0:T(8,128)} %convolution_bitcast_fusion.7), dimensions={2} | reverse | bytes 4194304 | tf_op jit(solution)/shard_map/rev | solution.py:39
  248.6 17.7 %rev.69 = f32[8,256,256]{2,1,0:T(8,128)} reverse(f32[8,256,256]{2,1,0:T(8,128)} %convolution_bitcast_fusion.6), dimensions={2} | reverse | bytes 4194304 | tf_op jit(solution)/shard_map/rev | solution.py:39
  268.2 17.7 %rev.70 = f32[8,256,256]{2,1,0:T(8,128)} reverse(f32[8,256,256]{2,1,0:T(8,128)} %convolution_bitcast_fusion.5), dimensions={2} | reverse | bytes 4194304 | tf_op jit(solution)/shard_map/rev | solution.py:39
  287.7 17.6 %rev.71 = f32[8,256,256]{2,1,0:T(8,128)} reverse(f32[8,256,256]{2,1,0:T(8,128)} %convolution_bitcast_fusion.4), dimensions={2} | reverse | bytes 4194304 | tf_op jit(solution)/shard_map/rev | solution.py:39
  305.8 11.6 %rev.72 = f32[8,256,256]{2,1,0:T(8,128)} reverse(f32[8,256,256]{2,1,0:T(8,128)S(1)} %convolution_bitcast_fusion.14), dimensions={2} | reverse | bytes 4194304 | tf_op jit(solution)/shard_map/rev | solution.py:39
  319.1 11.6 %rev.73 = f32[8,256,256]{2,1,0:T(8,128)} reverse(f32[8,256,256]{2,1,0:T(8,128)S(1)} %convolution_bitcast_fusion.3), dimensions={2} | reverse | bytes 4194304 | tf_op jit(solution)/shard_map/rev | solution.py:39
  331.2 11.6 %rev.74 = f32[8,256,256]{2,1,0:T(8,128)} reverse(f32[8,256,256]{2,1,0:T(8,128)S(1)} %convolution_bitcast_fusion.2), dimensions={2} | reverse | bytes 4194304 | tf_op jit(solution)/shard_map/rev | solution.py:39
  343.3 11.6 %rev.75 = f32[8,256,256]{2,1,0:T(8,128)} reverse(f32[8,256,256]{2,1,0:T(8,128)S(1)} %convolution_bitcast_fusion.1), dimensions={2} | reverse | bytes 4194304 | tf_op jit(solution)/shard_map/rev | solution.py:39
  355.4 11.6 %rev.76 = f32[8,256,256]{2,1,0:T(8,128)} reverse(f32[8,256,256]{2,1,0:T(8,128)S(1)} %convolution_bitcast_fusion.13), dimensions={2} | reverse | bytes 4194304 | tf_op jit(solution)/shard_map/rev | solution.py:39
  367.5 11.6 %rev.77 = f32[8,256,256]{2,1,0:T(8,128)} reverse(f32[8,256,256]{2,1,0:T(8,128)S(1)} %convolution_bitcast_fusion.12), dimensions={2} | reverse | bytes 4194304 | tf_op jit(solution)/shard_map/rev | solution.py:39
  379.6 11.6 %rev.78 = f32[8,256,256]{2,1,0:T(8,128)} reverse(f32[8,256,256]{2,1,0:T(8,128)S(1)} %convolution_bitcast_fusion), dimensions={2} | reverse | bytes 4194304 | tf_op jit(solution)/shard_map/rev | solution.py:39
  391.7 11.8 %rev.79 = f32[8,256,256]{2,1,0:T(8,128)} reverse(f32[8,256,256]{2,1,0:T(8,128)S(1)} %fusion.81), dimensions={2} | reverse | bytes 4194304 | tf_op jit(solution)/shard_map/rev | solution.py:39
  407.8 7.1 reshape.447
  424.9 7.1 reshape.445
  442.0 7.1 reshape.443
  459.2 7.3 reshape.441
  476.5 7.1 reshape.439
  493.6 7.1 reshape.437
  510.7 7.5 reshape.435
  528.2 7.1 reshape.433
  545.4 7.1 reshape.431
  562.5 7.1 reshape.429
  579.7 7.1 reshape.427
  596.9 7.1 reshape.425
  614.0 7.1 reshape.423
  631.1 7.3 reshape.421
  648.4 7.1 reshape.417
  665.5 7.1 reshape.419
  681.1 65.4 %all-reduce.65.cloned.1.call-done = f32[8,4096]{1,0:T(8,128)} async-done(((f32[8,4096]{1,0:T(8,128)}), f32[8,4096]{1,0:T(8,128)}) %all-reduce.65.cloned.1.call-update) | async-done | bytes 131088 | tf_op jit(solution)/shard_map/psum | solution.py:129
  777.8 5.3 reshape.406
  804.9 5.2 reshape.404
  855.1 5.2 reshape.401
  889.7 5.2 reshape.415
  922.0 5.4 reshape.412
  986.0 5.2 reshape.408
  1005.3 7.7 fusion.36
  1025.2 5.8 fusion.35
  1041.0 29.5 %all_to_all.81 = bf16[32,128,128]{2,1,0:T(8,128)(2,1)S(1)} all-to-all(bf16[32,128,128]{2,1,0:T(8,128)(2,1)S(1)} %get-tuple-element.60), channel_id=1, replica_groups=mesh['dp'=8,'ctx'=32] {'ctx'}, dimensions={0} | all-to-all | bytes 2097152 | tf_op jit(solution)/shard_map/all_to_all | solution.py:124
  1070.5 20.7 %all_to_all.82 = bf16[32,128,128]{2,1,0:T(8,128)(2,1)S(1)} all-to-all(bf16[32,128,128]{2,1,0:T(8,128)(2,1)S(1)} %get-tuple-element.61), channel_id=1, replica_groups=mesh['dp'=8,'ctx'=32] {'ctx'}, dimensions={0} | all-to-all | bytes 2097152 | tf_op jit(solution)/shard_map/all_to_all | solution.py:123
  1100.7 11.7 %all-to-all-done.5 = bf16[32,128,128]{2,1,0:T(8,128)(2,1)S(1)} async-done(((bf16[32,128,128]{2,1,0:T(8,128)(2,1)}), bf16[32,128,128]{2,1,0:T(8,128)(2,1)S(1)}, u32[]{:S(2)}, u32[]{:S(2)}) %all-to-all-start.5) | async-done | bytes 1048608 | tf_op jit(solution)/shard_map/all_to_all | solution.py:125
  (595 shorter events, 544.4 us)
Async XLA Ops:
  11.2 8.7 copy-start.74
  11.2 25.9 %all-to-all-start.1 = ((bf16[128,32,128]{2,0,1:T(8,128)(2,1)}), bf16[128,32,128]{2,0,1:T(8,128)(2,1)S(1)}, u32[]{:S(2)}, u32[]{:S(2)}) async-start(bf16[128,32,128]{2,0,1:T(8,128)(2,1)} %copy.207), calls=%async_computation.1 | async-start | bytes 2097152 | tf_op jit(solution)/shard_map/all_to_all | solution.py:109
  37.1 21.3 %all-to-all-start = ((bf16[128,32,128]{2,0,1:T(8,128)(2,1)}), bf16[128,32,128]{2,0,1:T(8,128)(2,1)S(1)}, u32[]{:S(2)}, u32[]{:S(2)}) async-start(bf16[128,32,128]{2,0,1:T(8,128)(2,1)} %copy.204), calls=%async_computation | async-start | bytes 2097152 | tf_op jit(solution)/shard_map/all_to_all | solution.py:110
  58.4 22.0 %all-to-all-start.3 = ((bf16[128,32,128]{2,0,1:T(8,128)(2,1)}), bf16[128,32,128]{2,0,1:T(8,128)(2,1)}, u32[]{:S(2)}, u32[]{:S(2)}) async-start(bf16[128,32,128]{2,0,1:T(8,128)(2,1)} %copy.243), calls=%async_computation.3 | async-start | bytes 2097152 | tf_op jit(solution)/shard_map/all_to_all | solution.py:111
  63.0 683.4 %all-reduce.65.cloned.1.call-start = ((), (), s32[]{:S(2)}) async-start(), calls=%async_computation.6 | async-start | bytes 262144 | tf_op jit(solution)/shard_map/psum | solution.py:129
  63.3 19.1 %copy-start.79 = (pred[32]{0:T(512)(128)(4,1)}, pred[32]{0:T(512)(128)(4,1)S(1)}, u32[]{:S(2)}) copy-start(pred[32]{0:T(512)(128)(4,1)S(1)} %compare_and_fusion.1) | copy-start | bytes 100
  68.2 14.8 %copy-start.2 = (bf16[32,128,128]{2,1,0:T(8,128)(2,1)}, bf16[32,128,128]{2,1,0:T(8,128)(2,1)S(1)}, u32[]{:S(2)}) copy-start(bf16[32,128,128]{2,1,0:T(8,128)(2,1)S(1)} %gather_fusion) | copy-start | bytes 3145732
  85.8 305.4 %copy-start.75 = (bf16[256,8,16]{0,2,1:T(8,128)(2,1)}, bf16[256,8,16]{0,2,1:T(8,128)(2,1)S(1)}, u32[]{:S(2)}) copy-start(bf16[256,8,16]{0,2,1:T(8,128)(2,1)S(1)} %reshape.414) | copy-start | bytes 196612
  87.1 279.9 %copy-start.60 = (bf16[3,256,8,16]{1,0,3,2:T(4,128)(2,1)}, bf16[3,256,8,16]{1,0,3,2:T(4,128)(2,1)S(1)}, u32[]{:S(2)}) copy-start(bf16[3,256,8,16]{1,0,3,2:T(4,128)(2,1)S(1)} %slice.794) | copy-start | bytes 589828
  106.0 62.8 %copy-start.31 = (bf16[16,256,8,16]{1,0,3,2:T(8,128)(2,1)}, bf16[16,256,8,16]{1,0,3,2:T(8,128)(2,1)S(1)}, u32[]{:S(2)}) copy-start(bf16[16,256,8,16]{1,0,3,2:T(8,128)(2,1)S(1)} %reshape_reshape.4) | copy-start | bytes 3145732
  106.0 4.7 slice-start.15
  106.1 5.5 slice-start.16
  106.1 6.4 slice-start.17
  108.0 5.5 slice-start.18
  108.0 6.6 slice-start.19
  116.0 4.6 slice-start.22
  117.4 4.6 slice-start.23
  143.8 25.1 %copy-start.32 = (bf16[16,256,8,16]{1,0,3,2:T(8,128)(2,1)}, bf16[16,256,8,16]{1,0,3,2:T(8,128)(2,1)S(1)}, u32[]{:S(2)}) copy-start(bf16[16,256,8,16]{1,0,3,2:T(8,128)(2,1)S(1)} %convert_element_type.227) | copy-start | bytes 3145732
  170.7 17.7 %copy-start.35 = (bf16[14,256,8,16]{1,0,3,2:T(8,128)(2,1)S(1)}, bf16[14,256,8,16]{1,0,3,2:T(8,128)(2,1)}, u32[]{:S(2)}) copy-start(bf16[14,256,8,16]{1,0,3,2:T(8,128)(2,1)} %slice.695) | copy-start | bytes 2752516
  170.7 17.7 %copy-start.37 = (bf16[14,256,8,16]{1,0,3,2:T(8,128)(2,1)S(1)}, bf16[14,256,8,16]{1,0,3,2:T(8,128)(2,1)}, u32[]{:S(2)}) copy-start(bf16[14,256,8,16]{1,0,3,2:T(8,128)(2,1)} %slice.822) | copy-start | bytes 2752516
  190.2 17.7 %copy-start.38 = (bf16[13,256,8,16]{1,0,3,2:T(8,128)(2,1)S(1)}, bf16[13,256,8,16]{1,0,3,2:T(8,128)(2,1)}, u32[]{:S(2)}) copy-start(bf16[13,256,8,16]{1,0,3,2:T(8,128)(2,1)} %slice.704) | copy-start | bytes 2555908
  190.2 17.7 %copy-start.40 = (bf16[13,256,8,16]{1,0,3,2:T(8,128)(2,1)S(1)}, bf16[13,256,8,16]{1,0,3,2:T(8,128)(2,1)}, u32[]{:S(2)}) copy-start(bf16[13,256,8,16]{1,0,3,2:T(8,128)(2,1)} %slice.824) | copy-start | bytes 2555908
  209.7 17.7 %copy-start.41 = (bf16[12,256,8,16]{1,0,3,2:T(8,128)(2,1)S(1)}, bf16[12,256,8,16]{1,0,3,2:T(8,128)(2,1)}, u32[]{:S(2)}) copy-start(bf16[12,256,8,16]{1,0,3,2:T(8,128)(2,1)} %slice.713) | copy-start | bytes 2359300
  209.7 17.7 %copy-start.43 = (bf16[12,256,8,16]{1,0,3,2:T(8,128)(2,1)S(1)}, bf16[12,256,8,16]{1,0,3,2:T(8,128)(2,1)}, u32[]{:S(2)}) copy-start(bf16[12,256,8,16]{1,0,3,2:T(8,128)(2,1)} %slice.826) | copy-start | bytes 2359300
  229.2 17.7 %copy-start.44 = (bf16[11,256,8,16]{1,0,3,2:T(8,128)(2,1)S(1)}, bf16[11,256,8,16]{1,0,3,2:T(8,128)(2,1)}, u32[]{:S(2)}) copy-start(bf16[11,256,8,16]{1,0,3,2:T(8,128)(2,1)} %slice.722) | copy-start | bytes 2162692
  229.2 17.7 %copy-start.46 = (bf16[11,256,8,16]{1,0,3,2:T(8,128)(2,1)S(1)}, bf16[11,256,8,16]{1,0,3,2:T(8,128)(2,1)}, u32[]{:S(2)}) copy-start(bf16[11,256,8,16]{1,0,3,2:T(8,128)(2,1)} %slice.828) | copy-start | bytes 2162692
  248.6 17.7 %copy-start.47 = (bf16[10,256,8,16]{1,0,3,2:T(8,128)(2,1)S(1)}, bf16[10,256,8,16]{1,0,3,2:T(8,128)(2,1)}, u32[]{:S(2)}) copy-start(bf16[10,256,8,16]{1,0,3,2:T(8,128)(2,1)} %slice.731) | copy-start | bytes 1966084
  248.6 17.7 %copy-start.49 = (bf16[10,256,8,16]{1,0,3,2:T(8,128)(2,1)S(1)}, bf16[10,256,8,16]{1,0,3,2:T(8,128)(2,1)}, u32[]{:S(2)}) copy-start(bf16[10,256,8,16]{1,0,3,2:T(8,128)(2,1)} %slice.830) | copy-start | bytes 1966084
  268.1 17.7 %copy-start.51 = (bf16[9,256,8,16]{1,0,3,2:T(8,128)(2,1)S(1)}, bf16[9,256,8,16]{1,0,3,2:T(8,128)(2,1)}, u32[]{:S(2)}) copy-start(bf16[9,256,8,16]{1,0,3,2:T(8,128)(2,1)} %slice.740) | copy-start | bytes 1769476
  268.1 17.7 %copy-start.53 = (bf16[9,256,8,16]{1,0,3,2:T(8,128)(2,1)S(1)}, bf16[9,256,8,16]{1,0,3,2:T(8,128)(2,1)}, u32[]{:S(2)}) copy-start(bf16[9,256,8,16]{1,0,3,2:T(8,128)(2,1)} %slice.832) | copy-start | bytes 1769476
  287.7 17.6 %copy-start.55 = (bf16[8,256,8,16]{1,0,3,2:T(8,128)(2,1)S(1)}, bf16[8,256,8,16]{1,0,3,2:T(8,128)(2,1)}, u32[]{:S(2)}) copy-start(bf16[8,256,8,16]{1,0,3,2:T(8,128)(2,1)} %slice.749) | copy-start | bytes 1572868
  287.7 17.6 %copy-start.57 = (bf16[8,256,8,16]{1,0,3,2:T(8,128)(2,1)S(1)}, bf16[8,256,8,16]{1,0,3,2:T(8,128)(2,1)}, u32[]{:S(2)}) copy-start(bf16[8,256,8,16]{1,0,3,2:T(8,128)(2,1)} %slice.834) | copy-start | bytes 1572868
  319.0 11.7 %copy-start.62 = (bf16[6,256,8,16]{1,0,3,2:T(8,128)(2,1)S(1)}, bf16[6,256,8,16]{1,0,3,2:T(8,128)(2,1)}, u32[]{:S(2)}) copy-start(bf16[6,256,8,16]{1,0,3,2:T(8,128)(2,1)} %slice.767) | copy-start | bytes 1179652
  319.1 11.6 %copy-start.64 = (bf16[6,256,8,16]{1,0,3,2:T(8,128)(2,1)S(1)}, bf16[6,256,8,16]{1,0,3,2:T(8,128)(2,1)}, u32[]{:S(2)}) copy-start(bf16[6,256,8,16]{1,0,3,2:T(8,128)(2,1)} %slice.838) | copy-start | bytes 1179652
  331.2 11.6 %copy-start.66 = (bf16[5,256,8,16]{1,0,3,2:T(8,128)(2,1)S(1)}, bf16[5,256,8,16]{1,0,3,2:T(8,128)(2,1)}, u32[]{:S(2)}) copy-start(bf16[5,256,8,16]{1,0,3,2:T(8,128)(2,1)} %slice.776) | copy-start | bytes 983044
  331.2 11.6 %copy-start.68 = (bf16[5,256,8,16]{1,0,3,2:T(8,128)(2,1)S(1)}, bf16[5,256,8,16]{1,0,3,2:T(8,128)(2,1)}, u32[]{:S(2)}) copy-start(bf16[5,256,8,16]{1,0,3,2:T(8,128)(2,1)} %slice.840) | copy-start | bytes 983044
  343.3 11.6 %copy-start.71 = (bf16[4,256,8,16]{1,0,3,2:T(4,128)(2,1)S(1)}, bf16[4,256,8,16]{1,0,3,2:T(4,128)(2,1)}, u32[]{:S(2)}) copy-start(bf16[4,256,8,16]{1,0,3,2:T(4,128)(2,1)} %slice.785) | copy-start | bytes 786436
  343.3 11.6 %copy-start.72 = (bf16[4,256,8,16]{1,0,3,2:T(4,128)(2,1)S(1)}, bf16[4,256,8,16]{1,0,3,2:T(4,128)(2,1)}, u32[]{:S(2)}) copy-start(bf16[4,256,8,16]{1,0,3,2:T(4,128)(2,1)} %slice.842) | copy-start | bytes 786436
  355.4 11.6 %copy-start.61 = (bf16[3,256,8,16]{1,0,3,2:T(4,128)(2,1)S(1)}, bf16[3,256,8,16]{1,0,3,2:T(4,128)(2,1)}, u32[]{:S(2)}) copy-start(bf16[3,256,8,16]{1,0,3,2:T(4,128)(2,1)} %slice.844) | copy-start | bytes 589828
  367.5 11.6 %copy-start.69 = (bf16[2,256,8,16]{1,0,3,2:T(2,128)(2,1)S(1)}, bf16[2,256,8,16]{1,0,3,2:T(2,128)(2,1)}, u32[]{:S(2)}) copy-start(bf16[2,256,8,16]{1,0,3,2:T(2,128)(2,1)} %slice.803) | copy-start | bytes 393220
  367.5 11.6 %copy-start.70 = (bf16[2,256,8,16]{1,0,3,2:T(2,128)(2,1)S(1)}, bf16[2,256,8,16]{1,0,3,2:T(2,128)(2,1)}, u32[]{:S(2)}) copy-start(bf16[2,256,8,16]{1,0,3,2:T(2,128)(2,1)} %slice.846) | copy-start | bytes 393220
  379.6 11.6 %copy-start.76 = (bf16[256,8,16]{0,2,1:T(8,128)(2,1)S(1)}, bf16[256,8,16]{0,2,1:T(8,128)(2,1)}, u32[]{:S(2)}) copy-start(bf16[256,8,16]{0,2,1:T(8,128)(2,1)} %reshape.416) | copy-start | bytes 196612
  677.1 69.4 %copy-start.77 = (f32[8,4096]{1,0:T(8,128)S(1)}, f32[8,4096]{1,0:T(8,128)}, u32[]{:S(2)}) copy-start(f32[8,4096]{1,0:T(8,128)} %param.12) | copy-start | bytes 393220
  764.5 5.1 copy-start.58
  777.8 5.3 copy-start.54
  791.4 5.1 copy-start.50
  1005.3 7.7 copy-start.10
  1091.2 21.3 %all-to-all-start.5 = ((bf16[32,128,128]{2,1,0:T(8,128)(2,1)}), bf16[32,128,128]{2,1,0:T(8,128)(2,1)S(1)}, u32[]{:S(2)}, u32[]{:S(2)}) async-start(bf16[32,128,128]{2,1,0:T(8,128)(2,1)} %get-tuple-element.59), calls=%async_computation.5 | async-start | bytes 2097152 | tf_op jit(solution)/shard_map/all_to_all | solution.py:125
  (71 other events, 198.6 us)
Sparse Core Ops, SparseCore 0:
  680.6 65.8 all-reduce.64
where the time goes:
time: 1150 us; the launch traced here: 1130 us
  local copies, waits for them, and re-layouts  770 us (67%)
  waiting for transfers between devices  119 us (10%)
  matrix products  92.7 us (8%)
  other arithmetic  61.6 us (5%)
  blocking collectives  50.2 us (4%)
  starting transfers between devices  21.5 us (2%)
  between operations  15.9 us (1%)
    rev x16, local copies, waits for them, and re-layouts, diagonal_sums(): flipped = square[:, :, ::-1]  234 us
    unnamed x256, local copies, waits for them, and re-layouts  117 us
    reshape x16, local copies, waits for them, and re-layouts, diagonal_sums(): padded.reshape(groups, block_rows * (2 * block_rows + 1))  114 us
    reshape x16, local copies, waits for them, and re-layouts, toeplitz_tables(): flat.reshape(groups, block_rows, 2 * block_rows - 1)[:, :, :block_rows]  81.9 us
    slice x16, local copies, waits for them, and re-layouts, diagonal_sums(): padded.reshape(groups, block_rows * (2 * block_rows + 1))  71.3 us
    psum x1, waiting for transfers between devices, shards(): lag_total = lax.psum(lag_sums, 'dp')  65.4 us
    pad x16, local copies, waits for them, and re-layouts, diagonal_sums(): padded = jnp.pad(flipped, ((0, 0), (0, 0), (0, block_rows + 1)))  45.8 us
    reduce_sum x16, other arithmetic, diagonal_sums(): return jnp.sum(flat.reshape(groups, block_rows, 2 * block_rows), axis=1)  42.4 us
  transfers between devices with their start and end apart: 5, of which 5 were waited for; matrix products, arithmetic and copies ran while one was open for 1% of the time, Pallas kernels for 0%

commit v1 on v0

--- a/solution.py
+++ b/solution.py
@@ -126,7 +126,10 @@
     )
     key_grad = gate_product(returned_here, values_here)
     value_grad = gate_product(returned_here, keys_here)
-    lag_total = lax.psum(lag_sums, "dp")
+    devices, lag_total = (lax.axis_size("dp"), lag_sums)
+    for far in [1 << k for k in range(devices.bit_length() - 1)]:
+        swap = [(i, i ^ far) for i in range(devices)]
+        lag_total = lag_total + lax.ppermute(lag_total, "dp", swap)
     lag_mean = lag_total / lax.axis_size("dp")
     projection = jnp.sum(lag_mean * filter_taps, axis=1, keepdims=True)
     taps_grad = (

time: 1150 us -> 1090 us (0.948)
  waiting for transfers between devices: 119 us -> 64.8 us
  between operations: 15.9 us -> 2.46 us
  starting transfers between devices: 21.5 us -> 33 us
    psum x1 -> x0, waiting for transfers between devices: 65.4 us -> none  [shards(): lag_total = lax.psum(lag_sums, 'dp')]
  transfers between devices with their start and end apart: 5 -> 7, of which waited for: 5 -> 7; matrix products, arithmetic and copies ran while one was open for 1% -> 1% of each run, Pallas kernels for 0% -> 0%
where the time goes in v1:
time: 1090 us; the launch traced here: 1070 us
  local copies, waits for them, and re-layouts  771 us (71%)
  matrix products  92.9 us (9%)
  waiting for transfers between devices  64.8 us (6%)
  other arithmetic  59.2 us (5%)
  blocking collectives  46.3 us (4%)
  starting transfers between devices  33 us (3%)
    rev x16, local copies, waits for them, and re-layouts, diagonal_sums(): flipped = square[:, :, ::-1]  235 us
    unnamed x256, local copies, waits for them, and re-layouts  118 us
    reshape x16, local copies, waits for them, and re-layouts, diagonal_sums(): padded.reshape(groups, block_rows * (2 * block_rows + 1))  113 us
    reshape x16, local copies, waits for them, and re-layouts, toeplitz_tables(): flat.reshape(groups, block_rows, 2 * block_rows - 1)[:, :, :block_rows]  81.9 us
    slice x16, local copies, waits for them, and re-layouts, diagonal_sums(): padded.reshape(groups, block_rows * (2 * block_rows + 1))  71.4 us
    pad x16, local copies, waits for them, and re-layouts, diagonal_sums(): padded = jnp.pad(flipped, ((0, 0), (0, 0), (0, block_rows + 1)))  46.1 us
    reduce_sum x16, other arithmetic, diagonal_sums(): return jnp.sum(flat.reshape(groups, block_rows, 2 * block_rows), axis=1)  42.4 us
    dot_general x16, matrix products, backward_part(): jnp.einsum('grs,jrgc->jsgc', tables[lag_block], later, preferred_element_...  38.4 us
  transfers between devices with their start and end apart: 7, of which 7 were waited for; matrix products, arithmetic and copies ran while one was open for 1% of the time, Pallas kernels for 0%

profile of v1, /device:TPU:1, one launch (start us, length us, event | category | flops | bytes accessed | tf_op | source)
XLA Modules:
  0.0 1069.8 jit_solution(4418385223171102422)
XLA Ops:
  4.7 8.7 all-to-all-start.1
  15.4 15.2 %all-to-all-done.1 = bf16[128,32,128]{2,0,1:T(8,128)(2,1)S(1)} async-done(((bf16[128,32,128]{2,0,1:T(8,128)(2,1)}), bf16[128,32,128]{2,0,1:T(8,128)(2,1)S(1)}, u32[]{:S(2)}, u32[]{:S(2)}) %all-to-all-start.1) | async-done | bytes 1048608 | tf_op jit(solution)/shard_map/all_to_all | solution.py:109
  37.5 14.3 %all-to-all-done = bf16[128,32,128]{2,0,1:T(8,128)(2,1)S(1)} async-done(((bf16[128,32,128]{2,0,1:T(8,128)(2,1)}), bf16[128,32,128]{2,0,1:T(8,128)(2,1)S(1)}, u32[]{:S(2)}, u32[]{:S(2)}) %all-to-all-start) | async-done | bytes 1048608 | tf_op jit(solution)/shard_map/all_to_all | solution.py:110
  61.4 12.7 %all-to-all-done.3 = bf16[128,32,128]{2,0,1:T(8,128)(2,1)} async-done(((bf16[128,32,128]{2,0,1:T(8,128)(2,1)}), bf16[128,32,128]{2,0,1:T(8,128)(2,1)}, u32[]{:S(2)}, u32[]{:S(2)}) %all-to-all-start.3) | async-done | bytes 1048608 | tf_op jit(solution)/shard_map/all_to_all | solution.py:111
  145.1 17.5 %rev.65 = f32[8,256,256]{2,1,0:T(8,128)} reverse(f32[8,256,256]{2,1,0:T(8,128)} %convolution_bitcast_fusion.10), dimensions={2} | reverse | bytes 4194304 | tf_op jit(solution)/shard_map/rev | solution.py:39
  164.5 17.7 %rev.64 = f32[8,256,256]{2,1,0:T(8,128)} reverse(f32[8,256,256]{2,1,0:T(8,128)} %convolution_bitcast_fusion.11), dimensions={2} | reverse | bytes 4194304 | tf_op jit(solution)/shard_map/rev | solution.py:39
  184.0 17.7 %rev.66 = f32[8,256,256]{2,1,0:T(8,128)} reverse(f32[8,256,256]{2,1,0:T(8,128)} %convolution_bitcast_fusion.9), dimensions={2} | reverse | bytes 4194304 | tf_op jit(solution)/shard_map/rev | solution.py:39
  203.5 17.7 %rev.67 = f32[8,256,256]{2,1,0:T(8,128)} reverse(f32[8,256,256]{2,1,0:T(8,128)} %convolution_bitcast_fusion.8), dimensions={2} | reverse | bytes 4194304 | tf_op jit(solution)/shard_map/rev | solution.py:39
  223.1 17.7 %rev.68 = f32[8,256,256]{2,1,0:T(8,128)} reverse(f32[8,256,256]{2,1,0:T(8,128)} %convolution_bitcast_fusion.7), dimensions={2} | reverse | bytes 4194304 | tf_op jit(solution)/shard_map/rev | solution.py:39
  242.6 17.7 %rev.69 = f32[8,256,256]{2,1,0:T(8,128)} reverse(f32[8,256,256]{2,1,0:T(8,128)} %convolution_bitcast_fusion.6), dimensions={2} | reverse | bytes 4194304 | tf_op jit(solution)/shard_map/rev | solution.py:39
  262.2 17.7 %rev.70 = f32[8,256,256]{2,1,0:T(8,128)} reverse(f32[8,256,256]{2,1,0:T(8,128)} %convolution_bitcast_fusion.5), dimensions={2} | reverse | bytes 4194304 | tf_op jit(solution)/shard_map/rev | solution.py:39
  281.7 17.6 %rev.71 = f32[8,256,256]{2,1,0:T(8,128)} reverse(f32[8,256,256]{2,1,0:T(8,128)} %convolution_bitcast_fusion.4), dimensions={2} | reverse | bytes 4194304 | tf_op jit(solution)/shard_map/rev | solution.py:39
  299.8 11.6 %rev.72 = f32[8,256,256]{2,1,0:T(8,128)} reverse(f32[8,256,256]{2,1,0:T(8,128)S(1)} %convolution_bitcast_fusion.14), dimensions={2} | reverse | bytes 4194304 | tf_op jit(solution)/shard_map/rev | solution.py:39
  313.2 11.6 %rev.73 = f32[8,256,256]{2,1,0:T(8,128)} reverse(f32[8,256,256]{2,1,0:T(8,128)S(1)} %convolution_bitcast_fusion.3), dimensions={2} | reverse | bytes 4194304 | tf_op jit(solution)/shard_map/rev | solution.py:39
  325.3 11.6 %rev.74 = f32[8,256,256]{2,1,0:T(8,128)} reverse(f32[8,256,256]{2,1,0:T(8,128)S(1)} %convolution_bitcast_fusion.2), dimensions={2} | reverse | bytes 4194304 | tf_op jit(solution)/shard_map/rev | solution.py:39
  337.5 11.6 %rev.75 = f32[8,256,256]{2,1,0:T(8,128)} reverse(f32[8,256,256]{2,1,0:T(8,128)S(1)} %convolution_bitcast_fusion.1), dimensions={2} | reverse | bytes 4194304 | tf_op jit(solution)/shard_map/rev | solution.py:39
  349.6 11.6 %rev.76 = f32[8,256,256]{2,1,0:T(8,128)} reverse(f32[8,256,256]{2,1,0:T(8,128)S(1)} %convolution_bitcast_fusion.13), dimensions={2} | reverse | bytes 4194304 | tf_op jit(solution)/shard_map/rev | solution.py:39
  361.8 11.7 %rev.77 = f32[8,256,256]{2,1,0:T(8,128)} reverse(f32[8,256,256]{2,1,0:T(8,128)S(1)} %convolution_bitcast_fusion.12), dimensions={2} | reverse | bytes 4194304 | tf_op jit(solution)/shard_map/rev | solution.py:39
  373.9 11.7 %rev.78 = f32[8,256,256]{2,1,0:T(8,128)} reverse(f32[8,256,256]{2,1,0:T(8,128)S(1)} %convolution_bitcast_fusion), dimensions={2} | reverse | bytes 4194304 | tf_op jit(solution)/shard_map/rev | solution.py:39
  386.1 11.8 %rev.79 = f32[8,256,256]{2,1,0:T(8,128)} reverse(f32[8,256,256]{2,1,0:T(8,128)S(1)} %fusion.81), dimensions={2} | reverse | bytes 4194304 | tf_op jit(solution)/shard_map/rev | solution.py:39
  402.2 7.0 reshape.447
  419.3 7.0 reshape.445
  436.5 7.0 reshape.443
  453.6 7.2 reshape.441
  470.9 7.0 reshape.439
  488.1 7.0 reshape.437
  505.2 7.4 reshape.435
  522.7 7.0 reshape.433
  539.8 7.0 reshape.431
  557.0 7.0 reshape.429
  574.3 7.0 reshape.427
  591.4 7.0 reshape.425
  608.5 7.0 reshape.423
  625.6 7.2 reshape.421
  643.0 7.0 reshape.417
  660.1 7.0 reshape.419
  683.2 5.2 collective-permute-done.1
  688.4 6.5 collective-permute-start.2
  727.3 5.3 reshape.406
  754.4 5.2 reshape.404
  839.4 5.2 reshape.415
  871.7 5.4 reshape.412
  935.8 5.2 reshape.408
  955.2 7.7 fusion.36
  975.0 5.8 fusion.35
  990.8 25.6 %all_to_all.81 = bf16[32,128,128]{2,1,0:T(8,128)(2,1)S(1)} all-to-all(bf16[32,128,128]{2,1,0:T(8,128)(2,1)S(1)} %get-tuple-element.60), channel_id=1, replica_groups=mesh['dp'=8,'ctx'=32] {'ctx'}, dimensions={0} | all-to-all | bytes 2097152 | tf_op jit(solution)/shard_map/all_to_all | solution.py:124
  1016.4 20.7 %all_to_all.82 = bf16[32,128,128]{2,1,0:T(8,128)(2,1)S(1)} all-to-all(bf16[32,128,128]{2,1,0:T(8,128)(2,1)S(1)} %get-tuple-element.61), channel_id=1, replica_groups=mesh['dp'=8,'ctx'=32] {'ctx'}, dimensions={0} | all-to-all | bytes 2097152 | tf_op jit(solution)/shard_map/all_to_all | solution.py:123
  1046.6 11.7 %all-to-all-done.5 = bf16[32,128,128]{2,1,0:T(8,128)(2,1)S(1)} async-done(((bf16[32,128,128]{2,1,0:T(8,128)(2,1)}), bf16[32,128,128]{2,1,0:T(8,128)(2,1)S(1)}, u32[]{:S(2)}, u32[]{:S(2)}) %all-to-all-start.5) | async-done | bytes 1048608 | tf_op jit(solution)/shard_map/all_to_all | solution.py:125
  (600 shorter events, 558.9 us)
Async XLA Ops:
  4.7 8.7 copy-start.74
  4.7 25.9 %all-to-all-start.1 = ((bf16[128,32,128]{2,0,1:T(8,128)(2,1)}), bf16[128,32,128]{2,0,1:T(8,128)(2,1)S(1)}, u32[]{:S(2)}, u32[]{:S(2)}) async-start(bf16[128,32,128]{2,0,1:T(8,128)(2,1)} %copy.207), calls=%async_computation.1 | async-start | bytes 2097152 | tf_op jit(solution)/shard_map/all_to_all | solution.py:109
  30.6 21.3 %all-to-all-start = ((bf16[128,32,128]{2,0,1:T(8,128)(2,1)}), bf16[128,32,128]{2,0,1:T(8,128)(2,1)S(1)}, u32[]{:S(2)}, u32[]{:S(2)}) async-start(bf16[128,32,128]{2,0,1:T(8,128)(2,1)} %copy.204), calls=%async_computation | async-start | bytes 2097152 | tf_op jit(solution)/shard_map/all_to_all | solution.py:110
  36.2 20.7 %copy-start.82 = (s32[32]{0:T(128)S(1)}, s32[32]{0:T(128)}, u32[]{:S(2)}) copy-start(s32[32]{0:T(128)} %param.13) | copy-start | bytes 388
  51.9 22.2 %all-to-all-start.3 = ((bf16[128,32,128]{2,0,1:T(8,128)(2,1)}), bf16[128,32,128]{2,0,1:T(8,128)(2,1)}, u32[]{:S(2)}, u32[]{:S(2)}) async-start(bf16[128,32,128]{2,0,1:T(8,128)(2,1)} %copy.243), calls=%async_computation.3 | async-start | bytes 2097152 | tf_op jit(solution)/shard_map/all_to_all | solution.py:111
  57.0 19.0 %copy-start.79 = (pred[32]{0:T(512)(128)(4,1)}, pred[32]{0:T(512)(128)(4,1)S(1)}, u32[]{:S(2)}) copy-start(pred[32]{0:T(512)(128)(4,1)S(1)} %compare_and_fusion.1) | copy-start | bytes 100
  61.4 15.3 %copy-start.2 = (bf16[32,128,128]{2,1,0:T(8,128)(2,1)}, bf16[32,128,128]{2,1,0:T(8,128)(2,1)S(1)}, u32[]{:S(2)}) copy-start(bf16[32,128,128]{2,1,0:T(8,128)(2,1)S(1)} %gather_fusion) | copy-start | bytes 3145732
  79.5 306.0 %copy-start.75 = (bf16[256,8,16]{0,2,1:T(8,128)(2,1)}, bf16[256,8,16]{0,2,1:T(8,128)(2,1)S(1)}, u32[]{:S(2)}) copy-start(bf16[256,8,16]{0,2,1:T(8,128)(2,1)S(1)} %reshape.414) | copy-start | bytes 196612
  80.8 280.4 %copy-start.60 = (bf16[3,256,8,16]{1,0,3,2:T(4,128)(2,1)}, bf16[3,256,8,16]{1,0,3,2:T(4,128)(2,1)S(1)}, u32[]{:S(2)}) copy-start(bf16[3,256,8,16]{1,0,3,2:T(4,128)(2,1)S(1)} %slice.794) | copy-start | bytes 589828
  99.8 62.9 %copy-start.31 = (bf16[16,256,8,16]{1,0,3,2:T(8,128)(2,1)}, bf16[16,256,8,16]{1,0,3,2:T(8,128)(2,1)S(1)}, u32[]{:S(2)}) copy-start(bf16[16,256,8,16]{1,0,3,2:T(8,128)(2,1)S(1)} %reshape_reshape.4) | copy-start | bytes 3145732
  99.8 5.5 slice-start.16
  99.8 6.4 slice-start.17
  101.8 5.5 slice-start.18
  101.8 6.6 slice-start.19
  137.5 25.2 %copy-start.32 = (bf16[16,256,8,16]{1,0,3,2:T(8,128)(2,1)}, bf16[16,256,8,16]{1,0,3,2:T(8,128)(2,1)S(1)}, u32[]{:S(2)}) copy-start(bf16[16,256,8,16]{1,0,3,2:T(8,128)(2,1)S(1)} %convert_element_type.227) | copy-start | bytes 3145732
  164.5 17.7 %copy-start.35 = (bf16[14,256,8,16]{1,0,3,2:T(8,128)(2,1)S(1)}, bf16[14,256,8,16]{1,0,3,2:T(8,128)(2,1)}, u32[]{:S(2)}) copy-start(bf16[14,256,8,16]{1,0,3,2:T(8,128)(2,1)} %slice.695) | copy-start | bytes 2752516
  164.5 17.7 %copy-start.37 = (bf16[14,256,8,16]{1,0,3,2:T(8,128)(2,1)S(1)}, bf16[14,256,8,16]{1,0,3,2:T(8,128)(2,1)}, u32[]{:S(2)}) copy-start(bf16[14,256,8,16]{1,0,3,2:T(8,128)(2,1)} %slice.822) | copy-start | bytes 2752516
  184.0 17.7 %copy-start.38 = (bf16[13,256,8,16]{1,0,3,2:T(8,128)(2,1)S(1)}, bf16[13,256,8,16]{1,0,3,2:T(8,128)(2,1)}, u32[]{:S(2)}) copy-start(bf16[13,256,8,16]{1,0,3,2:T(8,128)(2,1)} %slice.704) | copy-start | bytes 2555908
  184.0 17.7 %copy-start.40 = (bf16[13,256,8,16]{1,0,3,2:T(8,128)(2,1)S(1)}, bf16[13,256,8,16]{1,0,3,2:T(8,128)(2,1)}, u32[]{:S(2)}) copy-start(bf16[13,256,8,16]{1,0,3,2:T(8,128)(2,1)} %slice.824) | copy-start | bytes 2555908
  203.5 17.7 %copy-start.41 = (bf16[12,256,8,16]{1,0,3,2:T(8,128)(2,1)S(1)}, bf16[12,256,8,16]{1,0,3,2:T(8,128)(2,1)}, u32[]{:S(2)}) copy-start(bf16[12,256,8,16]{1,0,3,2:T(8,128)(2,1)} %slice.713) | copy-start | bytes 2359300
  203.5 17.7 %copy-start.43 = (bf16[12,256,8,16]{1,0,3,2:T(8,128)(2,1)S(1)}, bf16[12,256,8,16]{1,0,3,2:T(8,128)(2,1)}, u32[]{:S(2)}) copy-start(bf16[12,256,8,16]{1,0,3,2:T(8,128)(2,1)} %slice.826) | copy-start | bytes 2359300
  223.1 17.7 %copy-start.44 = (bf16[11,256,8,16]{1,0,3,2:T(8,128)(2,1)S(1)}, bf16[11,256,8,16]{1,0,3,2:T(8,128)(2,1)}, u32[]{:S(2)}) copy-start(bf16[11,256,8,16]{1,0,3,2:T(8,128)(2,1)} %slice.722) | copy-start | bytes 2162692
  223.1 17.7 %copy-start.46 = (bf16[11,256,8,16]{1,0,3,2:T(8,128)(2,1)S(1)}, bf16[11,256,8,16]{1,0,3,2:T(8,128)(2,1)}, u32[]{:S(2)}) copy-start(bf16[11,256,8,16]{1,0,3,2:T(8,128)(2,1)} %slice.828) | copy-start | bytes 2162692
  242.6 17.7 %copy-start.47 = (bf16[10,256,8,16]{1,0,3,2:T(8,128)(2,1)S(1)}, bf16[10,256,8,16]{1,0,3,2:T(8,128)(2,1)}, u32[]{:S(2)}) copy-start(bf16[10,256,8,16]{1,0,3,2:T(8,128)(2,1)} %slice.731) | copy-start | bytes 1966084
  242.6 17.7 %copy-start.49 = (bf16[10,256,8,16]{1,0,3,2:T(8,128)(2,1)S(1)}, bf16[10,256,8,16]{1,0,3,2:T(8,128)(2,1)}, u32[]{:S(2)}) copy-start(bf16[10,256,8,16]{1,0,3,2:T(8,128)(2,1)} %slice.830) | copy-start | bytes 1966084
  262.2 17.7 %copy-start.51 = (bf16[9,256,8,16]{1,0,3,2:T(8,128)(2,1)S(1)}, bf16[9,256,8,16]{1,0,3,2:T(8,128)(2,1)}, u32[]{:S(2)}) copy-start(bf16[9,256,8,16]{1,0,3,2:T(8,128)(2,1)} %slice.740) | copy-start | bytes 1769476
  262.2 17.7 %copy-start.53 = (bf16[9,256,8,16]{1,0,3,2:T(8,128)(2,1)S(1)}, bf16[9,256,8,16]{1,0,3,2:T(8,128)(2,1)}, u32[]{:S(2)}) copy-start(bf16[9,256,8,16]{1,0,3,2:T(8,128)(2,1)} %slice.832) | copy-start | bytes 1769476
  281.7 17.6 %copy-start.55 = (bf16[8,256,8,16]{1,0,3,2:T(8,128)(2,1)S(1)}, bf16[8,256,8,16]{1,0,3,2:T(8,128)(2,1)}, u32[]{:S(2)}) copy-start(bf16[8,256,8,16]{1,0,3,2:T(8,128)(2,1)} %slice.749) | copy-start | bytes 1572868
  281.7 17.6 %copy-start.57 = (bf16[8,256,8,16]{1,0,3,2:T(8,128)(2,1)S(1)}, bf16[8,256,8,16]{1,0,3,2:T(8,128)(2,1)}, u32[]{:S(2)}) copy-start(bf16[8,256,8,16]{1,0,3,2:T(8,128)(2,1)} %slice.834) | copy-start | bytes 1572868
  313.2 11.7 %copy-start.62 = (bf16[6,256,8,16]{1,0,3,2:T(8,128)(2,1)S(1)}, bf16[6,256,8,16]{1,0,3,2:T(8,128)(2,1)}, u32[]{:S(2)}) copy-start(bf16[6,256,8,16]{1,0,3,2:T(8,128)(2,1)} %slice.767) | copy-start | bytes 1179652
  313.2 11.7 %copy-start.64 = (bf16[6,256,8,16]{1,0,3,2:T(8,128)(2,1)S(1)}, bf16[6,256,8,16]{1,0,3,2:T(8,128)(2,1)}, u32[]{:S(2)}) copy-start(bf16[6,256,8,16]{1,0,3,2:T(8,128)(2,1)} %slice.838) | copy-start | bytes 1179652
  325.3 11.6 %copy-start.66 = (bf16[5,256,8,16]{1,0,3,2:T(8,128)(2,1)S(1)}, bf16[5,256,8,16]{1,0,3,2:T(8,128)(2,1)}, u32[]{:S(2)}) copy-start(bf16[5,256,8,16]{1,0,3,2:T(8,128)(2,1)} %slice.776) | copy-start | bytes 983044
  325.3 11.6 %copy-start.68 = (bf16[5,256,8,16]{1,0,3,2:T(8,128)(2,1)S(1)}, bf16[5,256,8,16]{1,0,3,2:T(8,128)(2,1)}, u32[]{:S(2)}) copy-start(bf16[5,256,8,16]{1,0,3,2:T(8,128)(2,1)} %slice.840) | copy-start | bytes 983044
  337.5 11.7 %copy-start.71 = (bf16[4,256,8,16]{1,0,3,2:T(4,128)(2,1)S(1)}, bf16[4,256,8,16]{1,0,3,2:T(4,128)(2,1)}, u32[]{:S(2)}) copy-start(bf16[4,256,8,16]{1,0,3,2:T(4,128)(2,1)} %slice.785) | copy-start | bytes 786436
  337.5 11.6 %copy-start.72 = (bf16[4,256,8,16]{1,0,3,2:T(4,128)(2,1)S(1)}, bf16[4,256,8,16]{1,0,3,2:T(4,128)(2,1)}, u32[]{:S(2)}) copy-start(bf16[4,256,8,16]{1,0,3,2:T(4,128)(2,1)} %slice.842) | copy-start | bytes 786436
  349.6 11.6 %copy-start.61 = (bf16[3,256,8,16]{1,0,3,2:T(4,128)(2,1)S(1)}, bf16[3,256,8,16]{1,0,3,2:T(4,128)(2,1)}, u32[]{:S(2)}) copy-start(bf16[3,256,8,16]{1,0,3,2:T(4,128)(2,1)} %slice.844) | copy-start | bytes 589828
  361.7 11.7 %copy-start.69 = (bf16[2,256,8,16]{1,0,3,2:T(2,128)(2,1)S(1)}, bf16[2,256,8,16]{1,0,3,2:T(2,128)(2,1)}, u32[]{:S(2)}) copy-start(bf16[2,256,8,16]{1,0,3,2:T(2,128)(2,1)} %slice.803) | copy-start | bytes 393220
  361.8 11.7 %copy-start.70 = (bf16[2,256,8,16]{1,0,3,2:T(2,128)(2,1)S(1)}, bf16[2,256,8,16]{1,0,3,2:T(2,128)(2,1)}, u32[]{:S(2)}) copy-start(bf16[2,256,8,16]{1,0,3,2:T(2,128)(2,1)} %slice.846) | copy-start | bytes 393220
  373.9 11.7 %copy-start.76 = (bf16[256,8,16]{0,2,1:T(8,128)(2,1)S(1)}, bf16[256,8,16]{0,2,1:T(8,128)(2,1)}, u32[]{:S(2)}) copy-start(bf16[256,8,16]{0,2,1:T(8,128)(2,1)} %reshape.416) | copy-start | bytes 196612
  671.6 11.0 %copy-start.83 = (s32[32]{0:T(128)S(1)}, s32[32]{0:T(128)}, u32[]{:S(2)}) copy-start(s32[32]{0:T(128)} %param.13) | copy-start | bytes 388
  671.6 26.1 %copy-start.77 = (f32[8,4096]{1,0:T(8,128)S(1)}, f32[8,4096]{1,0:T(8,128)}, u32[]{:S(2)}) copy-start(f32[8,4096]{1,0:T(8,128)} %param.12) | copy-start | bytes 393220
  674.4 5.1 collective-permute-start
  679.6 8.9 collective-permute-start.1
  688.4 9.3 collective-permute-start.2
  727.3 5.3 copy-start.54
  740.9 5.1 copy-start.50
  955.1 7.7 copy-start.10
  1037.1 21.3 %all-to-all-start.5 = ((bf16[32,128,128]{2,1,0:T(8,128)(2,1)}), bf16[32,128,128]{2,1,0:T(8,128)(2,1)S(1)}, u32[]{:S(2)}, u32[]{:S(2)}) async-start(bf16[32,128,128]{2,1,0:T(8,128)(2,1)} %get-tuple-element.59), calls=%async_computation.5 | async-start | bytes 2097152 | tf_op jit(solution)/shard_map/all_to_all | solution.py:125
  (73 other events, 211.3 us)
